TPU v7x, 128 devices: a whole 4x4x4 slice. The times are simulated.
128 devices in a mesh: lat: 4 (over z), lon: 32 (over x, y, core).
Axes of the slice: x: 4, y: 4, z: 4, core: 2. Of those that a mesh axis runs over, the one named last changes fastest.
Arguments:
- fields: bfloat16 [4, 69, 96, 4096], P(None, None, 'lat', 'lon'), may hold values from -6 to 6
- conv_weight: bfloat16 [9, 128, 69], replicated, may hold values from -0.25 to 0.25
- kv_weight: bfloat16 [512, 128], replicated, may hold values from -0.5 to 0.5
- out_weight: bfloat16 [256, 256], replicated, may hold values from -0.375 to 0.375
- norm_gain: float32 [256], replicated, may hold values from 0.5 to 1.5
- queries: bfloat16 [256, 256], replicated, may hold values from -64 to 64
Outputs:
- features: bfloat16 [4, 128, 96, 4096], P(None, None, 'lat', 'lon')
- latents: float32 [4, 256, 256], replicated
All inputs are finite; a program needn't handle non-finite values.
Results may differ from a plain program's by a relative error of at most 0.0035.
The roundings to bfloat16 on the way count: a program that leaves them out, or rounds other values in their place, can miss the bound.
Values may be sent and summed in bfloat16 or wider, within the bound.
A program may use at most 320 MiB of HBM per device.

v0:
```python
import jax
import jax.numpy as jnp
from jax import lax
from jax.sharding import PartitionSpec as P

DL = 256
Q = 256
HEADS = 4
HD = 64
BLK = 8


def extended(block, sides, width, periodic):
    for axis, dim in sides:
        count = lax.axis_size(axis)
        forward = [(i, i + 1) for i in range(count - 1)]
        if periodic:
            forward.append((count - 1, 0))
        backward = [(target, source) for source, target in forward]
        low = lax.ppermute(
            lax.slice_in_dim(block, block.shape[dim] - width, None, axis=dim), axis, forward
        )
        high = lax.ppermute(lax.slice_in_dim(block, 0, width, axis=dim), axis, backward)
        block = jnp.concatenate([low, block, high], axis=dim)
    return block


def convolve_block(window_in, conv_weight, lat_rows, lon_cols):
    running = jnp.zeros((window_in.shape[0], conv_weight.shape[1], lat_rows, lon_cols), jnp.float32)
    for tap_index in range(9):
        row_off = tap_index // 3
        col_off = tap_index % 3
        piece = window_in[:, :, row_off : row_off + lat_rows, col_off : col_off + lon_cols]
        running = running + jnp.einsum(
            "fc,bcin->bfin", conv_weight[tap_index], piece, preferred_element_type=jnp.float32
        )
    return running


def block_terms(window_in, conv_weight, kv_weight, queries, lat_rows, lon_cols):
    samples = window_in.shape[0]
    convolved = convolve_block(window_in, conv_weight, lat_rows, lon_cols)
    block_features = jax.nn.gelu(convolved, approximate=True).astype(jnp.bfloat16)
    flattened = block_features.reshape(samples, block_features.shape[1], lat_rows * lon_cols)
    key_value = jnp.einsum(
        "of,bfn->bon", kv_weight, flattened, preferred_element_type=jnp.float32
    ).astype(jnp.bfloat16)
    key_heads = key_value[:, :DL].reshape(samples, HEADS, HD, lat_rows * lon_cols)
    value_heads = key_value[:, DL:].reshape(samples, HEADS, HD, lat_rows * lon_cols)
    query_heads = queries.reshape(Q, HEADS, HD)
    scores = jnp.einsum(
        "qhd,bhdn->bhqn", query_heads, key_heads, preferred_element_type=jnp.float32
    ) * HD ** (-0.5)
    maxima = jnp.max(scores, axis=-1)
    exponent = jnp.exp(scores - maxima[..., None])
    totals = jnp.sum(exponent, axis=-1)
    weights_bf = exponent.astype(jnp.bfloat16)
    weighted = jnp.einsum(
        "bhqn,bhdn->bqhd", weights_bf, value_heads, preferred_element_type=jnp.float32
    )
    return (block_features, maxima, totals, weighted.reshape(samples, Q, DL))


def rescale(weighted, factor):
    full_shape = weighted.shape
    heads_view = weighted.reshape(full_shape[0], full_shape[1], factor.shape[1], -1)
    return (heads_view * jnp.transpose(factor, (0, 2, 1))[..., None]).reshape(full_shape)


def normalize(weighted, totals):
    full_shape = weighted.shape
    heads_view = weighted.reshape(full_shape[0], full_shape[1], totals.shape[1], -1)
    return (heads_view / jnp.transpose(totals, (0, 2, 1))[..., None]).reshape(full_shape)


def combine_partial(earlier, later):
    highest = jnp.maximum(earlier[0], later[0])
    scale_one = jnp.exp(earlier[0] - highest)
    scale_two = jnp.exp(later[0] - highest)
    totals = earlier[1] * scale_one + later[1] * scale_two
    weighted = rescale(earlier[2], scale_one) + rescale(later[2], scale_two)
    return (highest, totals, weighted)


def per_device(fields, conv_weight, kv_weight, out_weight, norm_gain, queries):
    samples, channels, lat_rows, lon_cols = fields.shape
    widened = extended(fields, (("lon", 3),), 1, True)
    padded = extended(widened, (("lat", 2),), 1, False)
    block_count = lat_rows // BLK
    initial = (
        jnp.full((samples, HEADS, Q), -1e30, jnp.float32),
        jnp.zeros((samples, HEADS, Q), jnp.float32),
        jnp.zeros((samples, Q, DL), jnp.float32),
    )

    def scan_step(running_state, block_index):
        zero_index = jnp.zeros((), jnp.int32)
        window_in = lax.dynamic_slice(
            padded,
            (zero_index, zero_index, block_index * BLK, zero_index),
            (samples, channels, BLK + 2, lon_cols + 2),
        )
        block_features, maxima, totals, weighted = block_terms(
            window_in, conv_weight, kv_weight, queries, BLK, lon_cols
        )
        return (combine_partial(running_state, (maxima, totals, weighted)), block_features)

    running_state, feats = lax.scan(scan_step, initial, jnp.arange(block_count, dtype=jnp.int32))
    features = jnp.transpose(feats, (1, 2, 0, 3, 4)).reshape(
        samples, feats.shape[2], lat_rows, lon_cols
    )
    maxima, totals, weighted = running_state
    peak = lax.pmax(maxima, ("lat", "lon"))
    factor = jnp.exp(maxima - peak)
    total_all, weighted_all = lax.psum((totals * factor, rescale(weighted, factor)), ("lat", "lon"))
    attended = normalize(weighted_all, total_all).astype(jnp.bfloat16)
    projected = jnp.einsum("bqe,ef->bqf", attended, out_weight, preferred_element_type=jnp.float32)
    latents = (
        projected
        * lax.rsqrt(jnp.mean(projected * projected, axis=-1, keepdims=True) + 1e-06)
        * norm_gain
    )
    return (features, latents)


def solution(mesh):
    in_specs = (P(None, None, "lat", "lon"), P(), P(), P(), P(), P())
    out_specs = (P(None, None, "lat", "lon"), P())
    return jax.shard_map(
        per_device, mesh=mesh, in_specs=in_specs, out_specs=out_specs, check_vma=False
    )
```

profile of v0, /device:TPU:1, one launch (start us, length us, event | category | flops | bytes accessed | tf_op | source)
XLA Modules:
  0.0 357.0 jit_solution(6077732282394592555)
XLA Ops:
  7.2 4.0 %fusion.74 = (bf16[4,69,24,1]{3,2,1,0:T(8,128)(2,1)}, bf16[4,69,24,1]{3,2,1,0:T(8,128)(2,1)S(1)}) fusion(bf16[4,69,24,128]{3,2,1,0:T(8,128)(2,1)} %param.8), kind=kLoop, calls=%fused_computation.92 | loop fusion | bytes 52992 | tf_op jit(solution)/shard_map/slice | solution.py:21
  11.2 2.2 copy.56
  13.4 2.8 collective-permute-start
  24.1 4.2 %collective-permute-start.2 = (bf16[4,69,1,130]{3,1,2,0:T(8,128)(2,1)S(1)}, bf16[4,69,1,130]{3,1,2,0:T(8,128)(2,1)}, u32[]{:S(2)}, u32[]{:S(2)}) collective-permute-start(bf16[4,69,1,130]{3,1,2,0:T(8,128)(2,1)S(1)} %get-tuple-element.150), channel_id=1, source_target_pairs={{0,32},{32,64},{64,96},{1,33},{33,65},{65,97},{2,34},{34,66},{66,9... | collective-permute-start | bytes 215288 | tf_op jit(solution)/shard_map/ppermute | solution.py:20
  29.8 4.5 %collective-permute-done.3 = bf16[4,69,1,130]{3,1,2,0:T(8,128)(2,1)} collective-permute-done((bf16[4,69,1,130]{3,1,2,0:T(8,128)(2,1)S(1)}, bf16[4,69,1,130]{3,1,2,0:T(8,128)(2,1)}, u32[]{:S(2)}, u32[]{:S(2)}) %collective-permute-start.3) | collective-permute-done | bytes 71792 | tf_op jit(solution)/shard_map/ppermute | solution.py:23
  34.3 5.1 %pad_maximum_fusion = bf16[4,69,26,130]{3,1,2,0:T(8,128)(2,1)} fusion(bf16[4,69,1,130]{3,1,2,0:T(8,128)(2,1)} %collective-permute-done.3, bf16[4,69,24,1]{3,1,2,0:T(8,128)(2,1)} %copy.32, bf16[4,69,24,128]{3,1,2,0:T(8,128)(2,1)S(1)} %copy.31, bf16[4,69,24,1]{3,1,2,0:T(8,128)(2,1)} %copy.30, bf16[4,69,1,130]{3,1,2,0:T(8,128)(2,1)} %collective-permute-done.2), kind=kLoop, calls=%fused_computation.76 | loop fusion | flops 9328800 | bytes 3731520 | tf_op jit(solution)/shard_map/concatenate | solution.py:24
  39.5 92.3 %while.17 = (s32[]{:T(128)}, f32[4,4,256]{2,0,1:T(4,128)}, f32[4,4,256]{2,0,1:T(4,128)}, f32[4,256,256]{1,2,0:T(8,128)S(1)}, bf16[3,4,128,8,128]{2,4,3,1,0:T(8,1...) while((s32[]{:T(128)}, f32[4,4,256]{2,0,1:T(4,128)}, ...), condition=%wide.region_3.4_spmd.clone, body=%wide.region_0.3_spmd.clone.sunk | while | flops 2299035648 | bytes 122200216 | solution.py:108
  42.9 2.1 fusion.136
  50.1 2.8 bitcast_dynamic-update-slice_fusion.2
  54.6 2.4 bitcast_reduce_fusion.2
  57.0 5.7 %fusion.144 = (bf16[4,4,256,1024]{2,3,0,1:T(8,128)(2,1)}, f32[4,4,256]{2,0,1:T(4,128)}) fusion(f32[4,4,1024,256]{3,2,1,0:T(8,128)S(1)} %get-tuple-element.235, f32[4,4,256]{2,0,1:T(4,128)S(1)} %get-tuple-element.233), kind=kLoop, calls=%fused_computation.3.clone.1 | loop fusion | flops 16773120 | bytes 25198592 | tf_op jit(solution)/shard_map/while/body/eval_jaxpr/convert_element_type | solution.py:57
  64.1 4.8 %fusion.146 = f32[4,256,4,64]{1,3,2,0:T(8,128)S(1)} fusion(bf16[4,4,64,1024]{3,2,1,0:T(8,128)(2,1)S(1)} %bitcast.183, bf16[4,4,256,1024]{2,3,0,1:T(8,128)(2,1)} %get-tuple-element.239, f32[4,256,4]{1,2,0:T(4,128)S(1)} %copy.74), kind=kOutput, calls=%fused_computation.20.clone.1 | convolution fusion | flops 537133056 | bytes 11550720 | tf_op jit(solution)/shard_map/while/body/eval_jaxpr/bhqn,bhdn->bqhd/dot_general | solution.py:58
  80.3 2.8 bitcast_dynamic-update-slice_fusion.2
  84.8 2.4 bitcast_reduce_fusion.2
  87.2 5.7 %fusion.144 = (bf16[4,4,256,1024]{2,3,0,1:T(8,128)(2,1)}, f32[4,4,256]{2,0,1:T(4,128)}) fusion(f32[4,4,1024,256]{3,2,1,0:T(8,128)S(1)} %get-tuple-element.235, f32[4,4,256]{2,0,1:T(4,128)S(1)} %get-tuple-element.233), kind=kLoop, calls=%fused_computation.3.clone.1 | loop fusion | flops 16773120 | bytes 25198592 | tf_op jit(solution)/shard_map/while/body/eval_jaxpr/convert_element_type | solution.py:57
  95.1 4.8 %fusion.146 = f32[4,256,4,64]{1,3,2,0:T(8,128)S(1)} fusion(bf16[4,4,64,1024]{3,2,1,0:T(8,128)(2,1)S(1)} %bitcast.183, bf16[4,4,256,1024]{2,3,0,1:T(8,128)(2,1)} %get-tuple-element.239, f32[4,256,4]{1,2,0:T(4,128)S(1)} %copy.74), kind=kOutput, calls=%fused_computation.20.clone.1 | convolution fusion | flops 537133056 | bytes 11550720 | tf_op jit(solution)/shard_map/while/body/eval_jaxpr/bhqn,bhdn->bqhd/dot_general | solution.py:58
  111.3 2.7 bitcast_dynamic-update-slice_fusion.2
  115.7 2.4 bitcast_reduce_fusion.2
  118.1 5.7 %fusion.144 = (bf16[4,4,256,1024]{2,3,0,1:T(8,128)(2,1)}, f32[4,4,256]{2,0,1:T(4,128)}) fusion(f32[4,4,1024,256]{3,2,1,0:T(8,128)S(1)} %get-tuple-element.235, f32[4,4,256]{2,0,1:T(4,128)S(1)} %get-tuple-element.233), kind=kLoop, calls=%fused_computation.3.clone.1 | loop fusion | flops 16773120 | bytes 25198592 | tf_op jit(solution)/shard_map/while/body/eval_jaxpr/convert_element_type | solution.py:57
  126.0 4.8 %fusion.146 = f32[4,256,4,64]{1,3,2,0:T(8,128)S(1)} fusion(bf16[4,4,64,1024]{3,2,1,0:T(8,128)(2,1)S(1)} %bitcast.183, bf16[4,4,256,1024]{2,3,0,1:T(8,128)(2,1)} %get-tuple-element.239, f32[4,256,4]{1,2,0:T(4,128)S(1)} %copy.74), kind=kOutput, calls=%fused_computation.20.clone.1 | convolution fusion | flops 537133056 | bytes 11550720 | tf_op jit(solution)/shard_map/while/body/eval_jaxpr/bhqn,bhdn->bqhd/dot_general | solution.py:58
  131.8 68.2 %pmax.7 = f32[4,4,256]{2,0,1:T(4,128)S(1)} all-reduce(f32[4,4,256]{2,0,1:T(4,128)} %get-tuple-element.59), channel_id=1, replica_groups=mesh['lat'=4,'lon'=32] {'lat','lon'}, use_global_device_ids=true, to_apply=%region_4.5 | all-reduce | flops 4096 | bytes 32768 | tf_op jit(solution)/shard_map/pmax | solution.py:113
  201.8 63.9 %psum.15 = f32[4,256,4]{1,0,2:T(4,128)S(1)} all-reduce(f32[4,256,4]{1,0,2:T(4,128)S(1)} %get-tuple-element.154), channel_id=1, replica_groups=mesh['lat'=4,'lon'=32] {'lat','lon'}, use_global_device_ids=true, to_apply=%region_6.7 | all-reduce | flops 4096 | bytes 32768 | tf_op jit(solution)/shard_map/psum | solution.py:115
  265.8 4.8 %copy.34 = bf16[4,128,3,8,128]{4,3,2,1,0:T(8,128)(2,1)} copy(bf16[4,128,3,8,128]{1,4,3,0,2:T(8,128)(2,1)} %bitcast.185) | data formatting | bytes 6291456 | tf_op jit(solution)/shard_map/transpose | solution.py:109
  270.6 76.4 %all-reduce.2.cloned.1.call-done = f32[4,256,256]{1,2,0:T(8,128)} async-done(((f32[4,256,256]{1,2,0:T(8,128)}), f32[4,256,256]{1,2,0:T(8,128)}) %all-reduce.2.cloned.1.call-update) | async-done | bytes 1048592 | tf_op jit(solution)/shard_map/psum | solution.py:115
  (109 shorter events, 54.9 us)
Async XLA Ops:
  7.2 341.1 %copy-start = (bf16[256,256]{1,0:T(8,128)(2,1)S(1)}, bf16[256,256]{1,0:T(8,128)(2,1)}, u32[]{:S(2)}) copy-start(bf16[256,256]{1,0:T(8,128)(2,1)} %param.11) | copy-start | bytes 393220
  7.2 339.8 %all-reduce.2.cloned.1.call-start = ((), (), s32[]{:S(2)}) async-start(), calls=%async_computation | async-start | bytes 2097152 | tf_op jit(solution)/shard_map/psum | solution.py:115
  13.4 5.7 %collective-permute-start = (bf16[4,69,24,1]{1,2,3,0:T(8,128)(2,1)S(1)}, bf16[4,69,24,1]{1,2,3,0:T(8,128)(2,1)S(1)}, u32[]{:S(2)}, u32[]{:S(2)}) collective-permute-start(bf16[4,69,24,1]{1,2,3,0:T(8,128)(2,1)S(1)} %copy.56), channel_id=1, source_target_pairs={{0,1},{1,2},{2,3},{3,4},{4,5},{5,6},{6,7},{7,8},{8,9},{9,10},{10,1... | collective-permute-start | bytes 39752 | tf_op jit(solution)/shard_map/ppermute | solution.py:20
  17.3 3.7 %collective-permute-start.1 = (bf16[4,69,24,1]{1,2,3,0:T(8,128)(2,1)S(1)}, bf16[4,69,24,1]{1,2,3,0:T(8,128)(2,1)S(1)}, u32[]{:S(2)}, u32[]{:S(2)}) collective-permute-start(bf16[4,69,24,1]{1,2,3,0:T(8,128)(2,1)S(1)} %copy.57), channel_id=1, source_target_pairs={{1,0},{2,1},{3,2},{4,3},{5,4},{6,5},{7,6},{8,7},{9,8},{10,9},{11,1... | collective-permute-start | bytes 39752 | tf_op jit(solution)/shard_map/ppermute | solution.py:23
  22.9 6.8 %copy-start.4 = (bf16[256,256]{1,0:T(8,128)(2,1)S(1)}, bf16[256,256]{1,0:T(8,128)(2,1)}, u32[]{:S(2)}) copy-start(bf16[256,256]{1,0:T(8,128)(2,1)} %param.13) | copy-start | bytes 393220
  24.1 5.7 %collective-permute-start.2 = (bf16[4,69,1,130]{3,1,2,0:T(8,128)(2,1)S(1)}, bf16[4,69,1,130]{3,1,2,0:T(8,128)(2,1)}, u32[]{:S(2)}, u32[]{:S(2)}) collective-permute-start(bf16[4,69,1,130]{3,1,2,0:T(8,128)(2,1)S(1)} %get-tuple-element.150), channel_id=1, source_target_pairs={{0,32},{32,64},{64,96},{1,33},{33,65},{65,97},{2,34},{34,66},{66,9... | collective-permute-start | bytes 215288 | tf_op jit(solution)/shard_map/ppermute | solution.py:20
  28.3 6.0 %collective-permute-start.3 = (bf16[4,69,1,130]{3,1,2,0:T(8,128)(2,1)S(1)}, bf16[4,69,1,130]{3,1,2,0:T(8,128)(2,1)}, u32[]{:S(2)}, u32[]{:S(2)}) collective-permute-start(bf16[4,69,1,130]{3,1,2,0:T(8,128)(2,1)S(1)} %get-tuple-element.151), channel_id=1, source_target_pairs={{32,0},{64,32},{96,64},{33,1},{65,33},{97,65},{34,2},{66,34},{98,6... | collective-permute-start | bytes 215288 | tf_op jit(solution)/shard_map/ppermute | solution.py:23
  29.8 9.7 %copy-start.3 = (bf16[512,128]{1,0:T(8,128)(2,1)S(1)}, bf16[512,128]{1,0:T(8,128)(2,1)}, u32[]{:S(2)}) copy-start(bf16[512,128]{1,0:T(8,128)(2,1)} %param.10) | copy-start | bytes 393220
  39.6 1.3 copy-start.6
  42.9 4.2 %copy-start.1 = (bf16[4,69,26,130]{3,1,2,0:T(8,128)(2,1)S(1)}, bf16[4,69,26,130]{3,1,2,0:T(8,128)(2,1)}, u32[]{:S(2)}) copy-start(bf16[4,69,26,130]{3,1,2,0:T(8,128)(2,1)} %get-tuple-element.281) | copy-start | bytes 5597284 | tf_op jit(solution)/shard_map/while
  42.9 4.2 %copy-start.2 = (bf16[9,128,69]{1,2,0:T(8,128)(2,1)S(1)}, bf16[9,128,69]{1,2,0:T(8,128)(2,1)}, u32[]{:S(2)}) copy-start(bf16[9,128,69]{1,2,0:T(8,128)(2,1)} %get-tuple-element.282) | copy-start | bytes 476932 | tf_op jit(solution)/shard_map/while
  68.9 1.0 copy-start.7
  69.9 1.2 copy-start.6
  73.2 4.2 %copy-start.1 = (bf16[4,69,26,130]{3,1,2,0:T(8,128)(2,1)S(1)}, bf16[4,69,26,130]{3,1,2,0:T(8,128)(2,1)}, u32[]{:S(2)}) copy-start(bf16[4,69,26,130]{3,1,2,0:T(8,128)(2,1)} %get-tuple-element.281) | copy-start | bytes 5597284 | tf_op jit(solution)/shard_map/while
  73.2 4.2 %copy-start.2 = (bf16[9,128,69]{1,2,0:T(8,128)(2,1)S(1)}, bf16[9,128,69]{1,2,0:T(8,128)(2,1)}, u32[]{:S(2)}) copy-start(bf16[9,128,69]{1,2,0:T(8,128)(2,1)} %get-tuple-element.282) | copy-start | bytes 476932 | tf_op jit(solution)/shard_map/while
  99.9 1.0 copy-start.7
  100.8 1.2 copy-start.6
  104.1 4.2 %copy-start.1 = (bf16[4,69,26,130]{3,1,2,0:T(8,128)(2,1)S(1)}, bf16[4,69,26,130]{3,1,2,0:T(8,128)(2,1)}, u32[]{:S(2)}) copy-start(bf16[4,69,26,130]{3,1,2,0:T(8,128)(2,1)} %get-tuple-element.281) | copy-start | bytes 5597284 | tf_op jit(solution)/shard_map/while
  104.1 4.2 %copy-start.2 = (bf16[9,128,69]{1,2,0:T(8,128)(2,1)S(1)}, bf16[9,128,69]{1,2,0:T(8,128)(2,1)}, u32[]{:S(2)}) copy-start(bf16[9,128,69]{1,2,0:T(8,128)(2,1)} %get-tuple-element.282) | copy-start | bytes 476932 | tf_op jit(solution)/shard_map/while
  130.8 1.0 copy-start.7
  270.6 78.1 %copy-start.5 = (f32[256]{0:T(256)S(1)}, f32[256]{0:T(256)}, u32[]{:S(2)}) copy-start(f32[256]{0:T(256)} %param.12) | copy-start | bytes 3076
Sparse Core Ops, SparseCore 0:
  201.9 144.9 all-reduce.1
where the time goes:
time: 358 us; the launch traced here: 357 us
  blocking collectives  132 us (37%)
  waiting for transfers between devices  80.9 us (23%)
  matrix products  61.3 us (17%)
  other arithmetic  33.4 us (9%)
  local copies, waits for them, and re-layouts  24.1 us (7%)
  between operations  14.2 us (4%)
  starting transfers between devices  8.37 us (2%)
    psum x1, waiting for transfers between devices, per_device(): lax.psum((totals * factor, rescale(weighted, factor)), ('lat', 'lon'))  76.4 us
    pmax x1, blocking collectives, per_device(): peak = lax.pmax(maxima, ('lat', 'lon'))  68.2 us
    psum x1, blocking collectives, per_device(): lax.psum((totals * factor, rescale(weighted, factor)), ('lat', 'lon'))  63.9 us
    dot_general x27, matrix products, convolve_block(): jnp.einsum('fc,bcin->bfin', conv_weight[tap_index], piece, preferred_elem...  35.6 us
    convert_element_type x3, other arithmetic, block_terms(): weights_bf = exponent.astype(jnp.bfloat16)  17.2 us
    dot_general x3, matrix products, block_terms(): jnp.einsum('bhqn,bhdn->bqhd', weights_bf, value_heads, preferred_element_...  14.4 us
    dot_general x3, matrix products, block_terms(): jnp.einsum('qhd,bhdn->bhqn', query_heads, key_heads, preferred_element_ty...  7.22 us
  transfers between devices with their start and end apart: 5, of which 2 were waited for; matrix products, arithmetic and copies ran while one was open for 3% of the time, Pallas kernels for 0%

commit v1 on v0

--- a/solution.py
+++ b/solution.py
@@ -112,7 +112,9 @@
     maxima, totals, weighted = running_state
     peak = lax.pmax(maxima, ("lat", "lon"))
     factor = jnp.exp(maxima - peak)
-    total_all, weighted_all = lax.psum((totals * factor, rescale(weighted, factor)), ("lat", "lon"))
+    total_all, weighted_all = lax.psum(
+        lax.psum((totals * factor, rescale(weighted, factor)), "lat"), "lon"
+    )
     attended = normalize(weighted_all, total_all).astype(jnp.bfloat16)
     projected = jnp.einsum("bqe,ef->bqf", attended, out_weight, preferred_element_type=jnp.float32)
     latents = (

time: 358 us -> 401 us (1.12); the launches traced: 357 us -> 395 us
  blocking collectives: 132 us -> 205 us
  waiting for transfers between devices: 80.9 us -> 46.7 us
    psum x1 -> x2, blocking collectives: 63.9 us -> 136 us  [the longest x1 124 us: per_device(): lax.psum(lax.psum((totals * factor, rescale(weighted, factor)), 'lat'), '...]
    psum x1 -> x2, waiting for transfers between devices: 76.4 us -> 42.2 us  [the longest x1 42.2 us: per_device(): lax.psum((totals * factor, rescale(weighted, factor)), 'lat')]
  transfers between devices with their start and end apart: 5 -> 6, of which waited for: 2 -> 2; matrix products, arithmetic and copies ran while one was open for 3% -> 2% of each run, Pallas kernels for 0% -> 0%
where the time goes in v1:
time: 401 us; the launch traced here: 395 us
  blocking collectives  205 us (51%)
  matrix products  61.3 us (15%)
  waiting for transfers between devices  46.7 us (12%)
  other arithmetic  33.4 us (8%)
  local copies, waits for them, and re-layouts  24.1 us (6%)
  between operations  14.2 us (4%)
  starting transfers between devices  8.39 us (2%)
    psum x1, blocking collectives, per_device(): lax.psum(lax.psum((totals * factor, rescale(weighted, factor)), 'lat'), '...  124 us
    pmax x1, blocking collectives, per_device(): peak = lax.pmax(maxima, ('lat', 'lon'))  68.2 us
    psum x1, waiting for transfers between devices, per_device(): lax.psum((totals * factor, rescale(weighted, factor)), 'lat')  42.2 us
    dot_general x27, matrix products, convolve_block(): jnp.einsum('fc,bcin->bfin', conv_weight[tap_index], piece, preferred_elem...  35.6 us
    convert_element_type x3, other arithmetic, block_terms(): weights_bf = exponent.astype(jnp.bfloat16)  17.1 us
    dot_general x3, matrix products, block_terms(): jnp.einsum('bhqn,bhdn->bqhd', weights_bf, value_heads, preferred_element_...  14.4 us
    psum x1, blocking collectives, per_device(): lax.psum((totals * factor, rescale(weighted, factor)), 'lat')  12.7 us
  transfers between devices with their start and end apart: 6, of which 2 were waited for; matrix products, arithmetic and copies ran while one was open for 2% of the time, Pallas kernels for 0%

profile of v1, /device:TPU:1, one launch (start us, length us, event | category | flops | bytes accessed | tf_op | source)
XLA Modules:
  0.0 395.2 jit_solution(5847579589919727448)
XLA Ops:
  7.2 4.0 %fusion.75 = (bf16[4,69,24,1]{3,2,1,0:T(8,128)(2,1)}, bf16[4,69,24,1]{3,2,1,0:T(8,128)(2,1)S(1)}) fusion(bf16[4,69,24,128]{3,2,1,0:T(8,128)(2,1)} %param.8), kind=kLoop, calls=%fused_computation.92 | loop fusion | bytes 52992 | tf_op jit(solution)/shard_map/slice | solution.py:21
  11.2 2.2 copy.56
  13.4 2.8 collective-permute-start
  24.1 4.2 %collective-permute-start.2 = (bf16[4,69,1,130]{3,1,2,0:T(8,128)(2,1)S(1)}, bf16[4,69,1,130]{3,1,2,0:T(8,128)(2,1)}, u32[]{:S(2)}, u32[]{:S(2)}) collective-permute-start(bf16[4,69,1,130]{3,1,2,0:T(8,128)(2,1)S(1)} %get-tuple-element.150), channel_id=1, source_target_pairs={{0,32},{32,64},{64,96},{1,33},{33,65},{65,97},{2,34},{34,66},{66,9... | collective-permute-start | bytes 215288 | tf_op jit(solution)/shard_map/ppermute | solution.py:20
  29.8 4.5 %collective-permute-done.3 = bf16[4,69,1,130]{3,1,2,0:T(8,128)(2,1)} collective-permute-done((bf16[4,69,1,130]{3,1,2,0:T(8,128)(2,1)S(1)}, bf16[4,69,1,130]{3,1,2,0:T(8,128)(2,1)}, u32[]{:S(2)}, u32[]{:S(2)}) %collective-permute-start.3) | collective-permute-done | bytes 71792 | tf_op jit(solution)/shard_map/ppermute | solution.py:23
  34.3 5.1 %pad_maximum_fusion = bf16[4,69,26,130]{3,1,2,0:T(8,128)(2,1)} fusion(bf16[4,69,1,130]{3,1,2,0:T(8,128)(2,1)} %collective-permute-done.3, bf16[4,69,24,1]{3,1,2,0:T(8,128)(2,1)} %copy.32, bf16[4,69,24,128]{3,1,2,0:T(8,128)(2,1)S(1)} %copy.31, bf16[4,69,24,1]{3,1,2,0:T(8,128)(2,1)} %copy.30, bf16[4,69,1,130]{3,1,2,0:T(8,128)(2,1)} %collective-permute-done.2), kind=kLoop, calls=%fused_computation.76 | loop fusion | flops 9328800 | bytes 3731520 | tf_op jit(solution)/shard_map/concatenate | solution.py:24
  39.4 92.2 %while.17 = (s32[]{:T(128)}, f32[4,4,256]{2,0,1:T(4,128)}, f32[4,4,256]{2,0,1:T(4,128)}, f32[4,256,256]{1,2,0:T(8,128)S(1)}, bf16[3,4,128,8,128]{2,4,3,1,0:T(8,1...) while((s32[]{:T(128)}, f32[4,4,256]{2,0,1:T(4,128)}, ...), condition=%wide.region_3.4_spmd.clone, body=%wide.region_0.3_spmd.clone.sunk | while | flops 2299035648 | bytes 122200216 | solution.py:108
  50.1 2.8 bitcast_dynamic-update-slice_fusion.2
  54.6 2.4 bitcast_reduce_fusion.2
  57.0 5.7 %fusion.145 = (bf16[4,4,256,1024]{2,3,0,1:T(8,128)(2,1)}, f32[4,4,256]{2,0,1:T(4,128)}) fusion(f32[4,4,1024,256]{3,2,1,0:T(8,128)S(1)} %get-tuple-element.235, f32[4,4,256]{2,0,1:T(4,128)S(1)} %get-tuple-element.233), kind=kLoop, calls=%fused_computation.3.clone.1 | loop fusion | flops 16773120 | bytes 25198592 | tf_op jit(solution)/shard_map/while/body/eval_jaxpr/convert_element_type | solution.py:57
  64.1 4.8 %fusion.147 = f32[4,256,4,64]{1,3,2,0:T(8,128)S(1)} fusion(bf16[4,4,64,1024]{3,2,1,0:T(8,128)(2,1)S(1)} %bitcast.182, bf16[4,4,256,1024]{2,3,0,1:T(8,128)(2,1)} %get-tuple-element.239, f32[4,256,4]{1,2,0:T(4,128)S(1)} %copy.74), kind=kOutput, calls=%fused_computation.20.clone.1 | convolution fusion | flops 537133056 | bytes 11550720 | tf_op jit(solution)/shard_map/while/body/eval_jaxpr/bhqn,bhdn->bqhd/dot_general | solution.py:58
  80.3 2.8 bitcast_dynamic-update-slice_fusion.2
  84.7 2.4 bitcast_reduce_fusion.2
  87.2 5.7 %fusion.145 = (bf16[4,4,256,1024]{2,3,0,1:T(8,128)(2,1)}, f32[4,4,256]{2,0,1:T(4,128)}) fusion(f32[4,4,1024,256]{3,2,1,0:T(8,128)S(1)} %get-tuple-element.235, f32[4,4,256]{2,0,1:T(4,128)S(1)} %get-tuple-element.233), kind=kLoop, calls=%fused_computation.3.clone.1 | loop fusion | flops 16773120 | bytes 25198592 | tf_op jit(solution)/shard_map/while/body/eval_jaxpr/convert_element_type | solution.py:57
  95.0 4.8 %fusion.147 = f32[4,256,4,64]{1,3,2,0:T(8,128)S(1)} fusion(bf16[4,4,64,1024]{3,2,1,0:T(8,128)(2,1)S(1)} %bitcast.182, bf16[4,4,256,1024]{2,3,0,1:T(8,128)(2,1)} %get-tuple-element.239, f32[4,256,4]{1,2,0:T(4,128)S(1)} %copy.74), kind=kOutput, calls=%fused_computation.20.clone.1 | convolution fusion | flops 537133056 | bytes 11550720 | tf_op jit(solution)/shard_map/while/body/eval_jaxpr/bhqn,bhdn->bqhd/dot_general | solution.py:58
  111.2 2.7 bitcast_dynamic-update-slice_fusion.2
  115.6 2.4 bitcast_reduce_fusion.2
  118.1 5.7 %fusion.145 = (bf16[4,4,256,1024]{2,3,0,1:T(8,128)(2,1)}, f32[4,4,256]{2,0,1:T(4,128)}) fusion(f32[4,4,1024,256]{3,2,1,0:T(8,128)S(1)} %get-tuple-element.235, f32[4,4,256]{2,0,1:T(4,128)S(1)} %get-tuple-element.233), kind=kLoop, calls=%fused_computation.3.clone.1 | loop fusion | flops 16773120 | bytes 25198592 | tf_op jit(solution)/shard_map/while/body/eval_jaxpr/convert_element_type | solution.py:57
  125.9 4.8 %fusion.147 = f32[4,256,4,64]{1,3,2,0:T(8,128)S(1)} fusion(bf16[4,4,64,1024]{3,2,1,0:T(8,128)(2,1)S(1)} %bitcast.182, bf16[4,4,256,1024]{2,3,0,1:T(8,128)(2,1)} %get-tuple-element.239, f32[4,256,4]{1,2,0:T(4,128)S(1)} %copy.74), kind=kOutput, calls=%fused_computation.20.clone.1 | convolution fusion | flops 537133056 | bytes 11550720 | tf_op jit(solution)/shard_map/while/body/eval_jaxpr/bhqn,bhdn->bqhd/dot_general | solution.py:58
  131.7 68.2 %pmax.7 = f32[4,4,256]{2,0,1:T(4,128)S(1)} all-reduce(f32[4,4,256]{2,0,1:T(4,128)} %get-tuple-element.59), channel_id=1, replica_groups=mesh['lat'=4,'lon'=32] {'lat','lon'}, use_global_device_ids=true, to_apply=%region_4.5 | all-reduce | flops 4096 | bytes 32768 | tf_op jit(solution)/shard_map/pmax | solution.py:113
  201.8 42.2 %all-reduce.3.cloned.1.call-done = f32[4,256,256]{1,2,0:T(8,128)} async-done(((f32[4,256,256]{1,2,0:T(8,128)}), f32[4,256,256]{1,2,0:T(8,128)}) %all-reduce.3.cloned.1.call-update) | async-done | bytes 1048592 | tf_op jit(solution)/shard_map/psum | solution.py:116
  244.0 12.7 %psum.30 = f32[4,4,256]{2,0,1:T(4,128)S(1)} all-reduce(f32[4,4,256]{2,0,1:T(4,128)S(1)} %get-tuple-element.154), channel_id=1, replica_groups=mesh['lat'=4,'lon'=32] {'lat'}, use_global_device_ids=true, to_apply=%region_7.8 | all-reduce | flops 4096 | bytes 32768 | tf_op jit(solution)/shard_map/psum | solution.py:116
  256.7 123.7 %psum.31 = f32[4,256,4]{1,0,2:T(4,128)S(1)} all-reduce(f32[4,256,4]{1,0,2:T(4,128)S(1)} %bitcast.186), channel_id=1, replica_groups=mesh['lat'=4,'lon'=32] {'lon'}, use_global_device_ids=true, to_apply=%region_8.9 | all-reduce | flops 4096 | bytes 32768 | tf_op jit(solution)/shard_map/psum | solution.py:115
  380.4 4.8 %copy.34 = bf16[4,128,3,8,128]{4,3,2,1,0:T(8,128)(2,1)} copy(bf16[4,128,3,8,128]{1,4,3,0,2:T(8,128)(2,1)} %bitcast.184) | data formatting | bytes 6291456 | tf_op jit(solution)/shard_map/transpose | solution.py:109
  (113 shorter events, 57.1 us)
Async XLA Ops:
  7.2 379.4 %copy-start = (bf16[256,256]{1,0:T(8,128)(2,1)S(1)}, bf16[256,256]{1,0:T(8,128)(2,1)}, u32[]{:S(2)}) copy-start(bf16[256,256]{1,0:T(8,128)(2,1)} %param.11) | copy-start | bytes 393220
  7.2 236.8 %all-reduce.3.cloned.1.call-start = ((), (), s32[]{:S(2)}) async-start(), calls=%async_computation | async-start | bytes 2097152 | tf_op jit(solution)/shard_map/psum | solution.py:116
  13.4 5.7 %collective-permute-start = (bf16[4,69,24,1]{1,2,3,0:T(8,128)(2,1)S(1)}, bf16[4,69,24,1]{1,2,3,0:T(8,128)(2,1)S(1)}, u32[]{:S(2)}, u32[]{:S(2)}) collective-permute-start(bf16[4,69,24,1]{1,2,3,0:T(8,128)(2,1)S(1)} %copy.56), channel_id=1, source_target_pairs={{0,1},{1,2},{2,3},{3,4},{4,5},{5,6},{6,7},{7,8},{8,9},{9,10},{10,1... | collective-permute-start | bytes 39752 | tf_op jit(solution)/shard_map/ppermute | solution.py:20
  17.3 3.7 collective-permute-start.1
  22.9 6.8 %copy-start.4 = (bf16[256,256]{1,0:T(8,128)(2,1)S(1)}, bf16[256,256]{1,0:T(8,128)(2,1)}, u32[]{:S(2)}) copy-start(bf16[256,256]{1,0:T(8,128)(2,1)} %param.13) | copy-start | bytes 393220
  24.1 5.7 %collective-permute-start.2 = (bf16[4,69,1,130]{3,1,2,0:T(8,128)(2,1)S(1)}, bf16[4,69,1,130]{3,1,2,0:T(8,128)(2,1)}, u32[]{:S(2)}, u32[]{:S(2)}) collective-permute-start(bf16[4,69,1,130]{3,1,2,0:T(8,128)(2,1)S(1)} %get-tuple-element.150), channel_id=1, source_target_pairs={{0,32},{32,64},{64,96},{1,33},{33,65},{65,97},{2,34},{34,66},{66,9... | collective-permute-start | bytes 215288 | tf_op jit(solution)/shard_map/ppermute | solution.py:20
  28.3 6.0 %collective-permute-start.3 = (bf16[4,69,1,130]{3,1,2,0:T(8,128)(2,1)S(1)}, bf16[4,69,1,130]{3,1,2,0:T(8,128)(2,1)}, u32[]{:S(2)}, u32[]{:S(2)}) collective-permute-start(bf16[4,69,1,130]{3,1,2,0:T(8,128)(2,1)S(1)} %get-tuple-element.151), channel_id=1, source_target_pairs={{32,0},{64,32},{96,64},{33,1},{65,33},{97,65},{34,2},{66,34},{98,6... | collective-permute-start | bytes 215288 | tf_op jit(solution)/shard_map/ppermute | solution.py:23
  29.8 9.7 %copy-start.3 = (bf16[512,128]{1,0:T(8,128)(2,1)S(1)}, bf16[512,128]{1,0:T(8,128)(2,1)}, u32[]{:S(2)}) copy-start(bf16[512,128]{1,0:T(8,128)(2,1)} %param.10) | copy-start | bytes 393220
  39.6 1.3 copy-start.6
  42.9 4.2 %copy-start.1 = (bf16[4,69,26,130]{3,1,2,0:T(8,128)(2,1)S(1)}, bf16[4,69,26,130]{3,1,2,0:T(8,128)(2,1)}, u32[]{:S(2)}) copy-start(bf16[4,69,26,130]{3,1,2,0:T(8,128)(2,1)} %get-tuple-element.281) | copy-start | bytes 5597284 | tf_op jit(solution)/shard_map/while
  42.9 4.2 %copy-start.2 = (bf16[9,128,69]{1,2,0:T(8,128)(2,1)S(1)}, bf16[9,128,69]{1,2,0:T(8,128)(2,1)}, u32[]{:S(2)}) copy-start(bf16[9,128,69]{1,2,0:T(8,128)(2,1)} %get-tuple-element.282) | copy-start | bytes 476932 | tf_op jit(solution)/shard_map/while
  68.9 1.0 copy-start.7
  69.9 1.2 copy-start.6
  73.1 4.2 %copy-start.1 = (bf16[4,69,26,130]{3,1,2,0:T(8,128)(2,1)S(1)}, bf16[4,69,26,130]{3,1,2,0:T(8,128)(2,1)}, u32[]{:S(2)}) copy-start(bf16[4,69,26,130]{3,1,2,0:T(8,128)(2,1)} %get-tuple-element.281) | copy-start | bytes 5597284 | tf_op jit(solution)/shard_map/while
  73.1 4.2 %copy-start.2 = (bf16[9,128,69]{1,2,0:T(8,128)(2,1)S(1)}, bf16[9,128,69]{1,2,0:T(8,128)(2,1)}, u32[]{:S(2)}) copy-start(bf16[9,128,69]{1,2,0:T(8,128)(2,1)} %get-tuple-element.282) | copy-start | bytes 476932 | tf_op jit(solution)/shard_map/while
  99.8 1.0 copy-start.7
  100.8 1.2 copy-start.6
  104.0 4.2 %copy-start.1 = (bf16[4,69,26,130]{3,1,2,0:T(8,128)(2,1)S(1)}, bf16[4,69,26,130]{3,1,2,0:T(8,128)(2,1)}, u32[]{:S(2)}) copy-start(bf16[4,69,26,130]{3,1,2,0:T(8,128)(2,1)} %get-tuple-element.281) | copy-start | bytes 5597284 | tf_op jit(solution)/shard_map/while
  104.0 4.2 %copy-start.2 = (bf16[9,128,69]{1,2,0:T(8,128)(2,1)S(1)}, bf16[9,128,69]{1,2,0:T(8,128)(2,1)}, u32[]{:S(2)}) copy-start(bf16[9,128,69]{1,2,0:T(8,128)(2,1)} %get-tuple-element.282) | copy-start | bytes 476932 | tf_op jit(solution)/shard_map/while
  130.7 1.0 copy-start.7
  201.7 183.5 %all-reduce.5.cloned.1.call-start = ((), (), s32[]{:S(2)}) async-start(), calls=%async_computation.1 | async-start | bytes 2097152 | tf_op jit(solution)/shard_map/psum | solution.py:115
  385.2 1.7 copy-start.5
Sparse Core Ops, SparseCore 0:
  201.8 42.0 all-reduce.2
  247.5 106.7 all-reduce.4
